TPU v7x, 32 devices: a whole 2x2x4 slice. The times are simulated.
32 devices in a mesh: aux: 4 (over z), ao: 8 (over y, x, core).
Axes of the slice: x: 2, y: 2, z: 4, core: 2. Of those that a mesh axis runs over, the one named last changes fastest.
Arguments:
- tensor: bfloat16 [64, 1024, 1024], P('aux', 'ao'), may hold values from -6 to 6
- green: bfloat16 [1024, 1024], P('aux', 'ao'), may hold values from -0.1875 to 0.1875
- tensor_mask: int32 [4, 8, 8], P('aux', 'ao'), may hold values 0 or 1
- green_mask: int32 [8, 8], P('aux', 'ao'), may hold values 0 or 1
Outputs:
- contracted: bfloat16 [64, 1024, 1024], P('aux', 'ao')
- polar: float32 [64, 16], P('aux')
All inputs are finite; a program needn't handle non-finite values. No bound on the sum of `tensor_mask` or of `green_mask` on one device may be relied on, other than what follows from the above.
Results may differ from a plain program's by a relative error of at most 0.001.
Values may be sent and summed in bfloat16 or wider, within the bound.
A program may use at most 128 MiB of HBM per device.

v0:
```python
import jax
import jax.numpy as jnp
from jax import lax
from jax.sharding import PartitionSpec as P

BLK = 128


def expand_blocks(mask, width):
    return jnp.repeat(jnp.repeat(mask, width, axis=0), width, axis=1)


def local(tensor, green, tensor_mask, green_mask):
    aux_count, row_count, orbitals = tensor.shape
    masked = tensor * expand_blocks(tensor_mask[0], BLK).astype(jnp.bfloat16)[None]
    green_local = green * expand_blocks(green_mask, BLK).astype(jnp.bfloat16)
    columns = lax.all_gather(green_local, "aux", axis=0, tiled=True)
    product = jnp.einsum(
        "pmn,nk->pmk",
        masked,
        lax.all_gather(columns, "ao", axis=1, tiled=True),
        preferred_element_type=jnp.float32,
    )
    flat_product = product.reshape(aux_count, row_count * orbitals)
    flat_masked = masked.reshape(aux_count, row_count * orbitals).astype(jnp.float32)
    partial_polar = jnp.dot(flat_product, flat_masked.T, precision=lax.Precision.HIGHEST)
    polar = lax.psum(partial_polar, "ao") / orbitals
    return (product.astype(jnp.bfloat16), polar)


def solution(mesh):
    return jax.shard_map(
        local,
        mesh=mesh,
        in_specs=(P("aux", "ao", None), P("aux", "ao"), P("aux", "ao", None), P("aux", "ao")),
        out_specs=(P("aux", "ao", None), P("aux", None)),
        check_vma=False,
    )
```

profile of v0, /device:TPU:0, one launch (start us, length us, event | category | flops | bytes accessed | tf_op | source)
XLA Modules:
  0.0 101.3 jit_solution(9471934883735907705)
XLA Ops:
  7.2 0.0 all-gather.2.cloned.1.call-start
  7.2 0.7 convert_bitcast_fusion
  7.9 0.1 broadcast_bitcast_fusion.1
  7.9 0.9 broadcast_multiply_fusion.1
  8.9 16.3 %all_gather.6 = bf16[1024,128]{1,0:T(8,128)(2,1)} all-gather(bf16[256,128]{1,0:T(8,128)(2,1)S(1)} %broadcast_multiply_fusion.1), channel_id=1, replica_groups=mesh['aux'=4,'ao'=8] {'aux'}, dimensions={0}, use_global_device_ids=true | all-gather | bytes 327680 | tf_op jit(solution)/shard_map/all_gather | solution.py:17
  25.2 0.0 all-gather.2.cloned.1.call-update
  25.2 0.7 convert_bitcast_fusion.1
  25.9 0.1 broadcast_bitcast_fusion
  26.0 4.4 %broadcast_multiply_fusion = bf16[16,128,1024]{2,1,0:T(8,128)(2,1)} fusion(bf16[16,128,1024]{2,1,0:T(8,128)(2,1)} %param.4, bf16[1024]{0:T(1024)(128)(2,1)S(1)} %broadcast_bitcast_fusion), kind=kLoop, calls=%fused_computation.5 | loop fusion | flops 2097152 | bytes 8390656 | tf_op jit(solution)/shard_map/mul | solution.py:15
  30.4 24.8 %all-gather.2.cloned.1.call-done = bf16[1024,1024]{1,0:T(8,128)(2,1)} async-done(((bf16[1024,128]{1,0:T(8,128)(2,1)}), bf16[1024,1024]{1,0:T(8,128)(2,1)}) %all-gather.2.cloned.1.call-update) | async-done | bytes 2097168 | tf_op jit(solution)/shard_map/all_gather | solution.py:21
  55.1 0.0 copy-start
  55.2 9.5 %fusion.10 = (bf16[16,128,1024]{2,1,0:T(8,128)(2,1)}, f32[16,128,1024]{2,1,0:T(8,128)S(1)}) fusion(bf16[16,128,1024]{2,1,0:T(8,128)(2,1)} %broadcast_multiply_fusion, bf16[1024,1024]{1,0:T(8,128)(2,1)} %all-gather.2.cloned.1.call-done), kind=kOutput, calls=%fused_computation.13 | convolution fusion | flops 4297064448 | bytes 18874368 | tf_op jit(solution)/shard_map/pmn,nk->pmk/dot_general | solution.py:18
  64.7 0.0 copy-done
  64.7 15.8 %fusion.5 = f32[16,16]{1,0:T(8,128)S(1)} fusion(bf16[16,128,1024]{2,1,0:T(8,128)(2,1)S(1)} %copy-done, f32[16,128,1024]{2,1,0:T(8,128)S(1)} %get-tuple-element.3), kind=kOutput, calls=%fused_computation.6 | convolution fusion | flops 402653184 | bytes 12583936 | tf_op jit(solution)/shard_map/dot_general | solution.py:26
  80.5 13.4 %psum.7 = f32[16,16]{1,0:T(8,128)S(1)} all-reduce(f32[16,16]{1,0:T(8,128)S(1)} %fusion.5), channel_id=1, replica_groups=mesh['aux'=4,'ao'=8] {'ao'}, use_global_device_ids=true, to_apply=%region_0.0 | all-reduce | flops 256 | bytes 2048 | tf_op jit(solution)/shard_map/psum | solution.py:27
  93.9 0.6 broadcast_multiply_fusion.2
Async XLA Ops:
  7.2 48.0 %all-gather.2.cloned.1.call-start = ((), (), s32[]{:S(2)}) async-start(), calls=%async_computation | async-start | bytes 2359296 | tf_op jit(solution)/shard_map/all_gather | solution.py:21
  55.1 9.5 %copy-start = (bf16[16,128,1024]{2,1,0:T(8,128)(2,1)S(1)}, bf16[16,128,1024]{2,1,0:T(8,128)(2,1)}, u32[]{:S(2)}) copy-start(bf16[16,128,1024]{2,1,0:T(8,128)(2,1)} %broadcast_multiply_fusion) | copy-start | bytes 12582916
Sparse Core Ops, SparseCore 0:
  25.3 29.7 all-gather.1
where the time goes:
time: 102 us; the launch traced here: 101 us
  blocking collectives  29.7 us (29%)
  matrix products  25.3 us (25%)
  waiting for transfers between devices  24.8 us (24%)
  between operations  14 us (14%)
  other arithmetic  7.25 us (7%)
    all_gather x1, waiting for transfers between devices, local(): lax.all_gather(columns, 'ao', axis=1, tiled=True)  24.8 us
    all_gather x1, blocking collectives, local(): columns = lax.all_gather(green_local, 'aux', axis=0, tiled=True)  16.3 us
    dot_general x1, matrix products, local(): jnp.dot(flat_product, flat_masked.T, precision=lax.Precision.HIGHEST)  15.8 us
    psum x1, blocking collectives, local(): polar = lax.psum(partial_polar, 'ao') / orbitals  13.4 us
    dot_general x1, matrix products, local(): jnp.einsum('pmn,nk->pmk', masked, lax.all_gather(columns, 'ao', axis=1, t...  9.54 us
    mul x1, other arithmetic, local(): tensor * expand_blocks(tensor_mask[0], BLK).astype(jnp.bfloat16)[None]  4.39 us
  transfers between devices with their start and end apart: 1, of which 1 were waited for; matrix products, arithmetic and copies ran while one was open for 5% of the time, Pallas kernels for 0%

commit v1 on v0

--- a/solution.py
+++ b/solution.py
@@ -4,6 +4,28 @@
 from jax.sharding import PartitionSpec as P
 
 BLK = 128
+
+
+def unit_open(block_here, ax_name, row_dim):
+    response, b_next, u_next = (
+        jax.lax.axis_size(ax_name),
+        jax.lax.axis_index(ax_name),
+        block_here.shape[row_dim],
+    )
+    frames = list(map(lambda i: (i, (i + 1) % response), range(response)))
+    earlier = jnp.zeros(
+        (*block_here.shape[:row_dim], response * u_next, *block_here.shape[row_dim + 1 :]),
+        block_here.dtype,
+    )
+    new = block_here
+    t = 0
+    while t < response:
+        r2 = (b_next - t) % response
+        earlier = lax.dynamic_update_slice_in_dim(earlier, new, r2 * u_next, axis=row_dim)
+        if t < response - 1:
+            new = jax.lax.ppermute(new, ax_name, frames)
+        t = t + 1
+    return earlier
 
 
 def expand_blocks(mask, width):
@@ -16,10 +38,7 @@
     green_local = green * expand_blocks(green_mask, BLK).astype(jnp.bfloat16)
     columns = lax.all_gather(green_local, "aux", axis=0, tiled=True)
     product = jnp.einsum(
-        "pmn,nk->pmk",
-        masked,
-        lax.all_gather(columns, "ao", axis=1, tiled=True),
-        preferred_element_type=jnp.float32,
+        "pmn,nk->pmk", masked, unit_open(columns, "ao", 1), preferred_element_type=jnp.float32
     )
     flat_product = product.reshape(aux_count, row_count * orbitals)
     flat_masked = masked.reshape(aux_count, row_count * orbitals).astype(jnp.float32)

time: 102 us -> 99.8 us (0.978)
  waiting for transfers between devices: 24.8 us -> 40.7 us
  between operations: 14 us -> 0.74 us
  matrix products: 25.3 us -> 21.9 us
  blocking collectives: 29.7 us -> 27.7 us
    ppermute x0 -> x7, waiting for transfers between devices: none -> 40.7 us  [unit_open(): new = jax.lax.ppermute(new, ax_name, frames)]
    all_gather x1 -> x0, waiting for transfers between devices: 24.8 us -> none  [local(): lax.all_gather(columns, 'ao', axis=1, tiled=True)]
    dot_general x1, matrix products: 9.54 us -> 6.09 us  [local(): jnp.einsum('pmn,nk->pmk', masked, unit_open(columns, 'ao', 1), preferred_...]
    psum x1, blocking collectives: 13.4 us -> 12.1 us  [local(): polar = lax.psum(partial_polar, 'ao') / orbitals]
  transfers between devices with their start and end apart: 1 -> 7, of which waited for: 1 -> 7; matrix products, arithmetic and copies ran while one was open for 5% -> 6% of each run, Pallas kernels for 0% -> 0%
where the time goes in v1:
time: 99.8 us; the launch traced here: 99.5 us
  waiting for transfers between devices  40.7 us (41%)
  blocking collectives  27.7 us (28%)
  matrix products  21.9 us (22%)
  other arithmetic  7.33 us (7%)
  local copies, waits for them, and re-layouts  1.1 us (1%)
    ppermute x7, waiting for transfers between devices, unit_open(): new = jax.lax.ppermute(new, ax_name, frames)  40.7 us
    dot_general x1, matrix products, local(): jnp.dot(flat_product, flat_masked.T, precision=lax.Precision.HIGHEST)  15.8 us
    all_gather x1, blocking collectives, local(): columns = lax.all_gather(green_local, 'aux', axis=0, tiled=True)  15.6 us
    psum x1, blocking collectives, local(): polar = lax.psum(partial_polar, 'ao') / orbitals  12.1 us
    dot_general x1, matrix products, local(): jnp.einsum('pmn,nk->pmk', masked, unit_open(columns, 'ao', 1), preferred_...  6.09 us
    mul x1, other arithmetic, local(): tensor * expand_blocks(tensor_mask[0], BLK).astype(jnp.bfloat16)[None]  4.47 us
  transfers between devices with their start and end apart: 7, of which 7 were waited for; matrix products, arithmetic and copies ran while one was open for 6% of the time, Pallas kernels for 0%

profile of v1, /device:TPU:0, one launch (start us, length us, event | category | flops | bytes accessed | tf_op | source)
XLA Modules:
  0.0 99.5 jit_solution(9172508954560843679)
XLA Ops:
  0.6 0.7 convert_bitcast_fusion
  1.3 0.1 broadcast_bitcast_fusion.1
  1.4 0.9 broadcast_multiply_fusion.1
  2.3 15.6 %all_gather.3 = bf16[1024,128]{1,0:T(8,128)(2,1)S(1)} all-gather(bf16[256,128]{1,0:T(8,128)(2,1)S(1)} %broadcast_multiply_fusion.1), channel_id=1, replica_groups=mesh['aux'=4,'ao'=8] {'aux'}, dimensions={0}, use_global_device_ids=true | all-gather | bytes 327680 | tf_op jit(solution)/shard_map/all_gather | solution.py:39
  17.9 0.0 collective-permute-start
  17.9 6.7 %collective-permute-done = bf16[1024,128]{1,0:T(8,128)(2,1)S(1)} collective-permute-done((bf16[1024,128]{1,0:T(8,128)(2,1)S(1)}, bf16[1024,128]{1,0:T(8,128)(2,1)S(1)}, u32[]{:S(2)}, u32[]{:S(2)}) %collective-permute-start) | collective-permute-done | bytes 262176 | tf_op jit(solution)/shard_map/ppermute | solution.py:26
  24.6 0.0 collective-permute-start.1
  24.6 6.7 %collective-permute-done.1 = bf16[1024,128]{1,0:T(8,128)(2,1)S(1)} collective-permute-done((bf16[1024,128]{1,0:T(8,128)(2,1)S(1)}, bf16[1024,128]{1,0:T(8,128)(2,1)S(1)}, u32[]{:S(2)}, u32[]{:S(2)}) %collective-permute-start.1) | collective-permute-done | bytes 262176 | tf_op jit(solution)/shard_map/ppermute | solution.py:26
  31.3 0.0 collective-permute-start.2
  31.3 6.7 %collective-permute-done.2 = bf16[1024,128]{1,0:T(8,128)(2,1)S(1)} collective-permute-done((bf16[1024,128]{1,0:T(8,128)(2,1)S(1)}, bf16[1024,128]{1,0:T(8,128)(2,1)S(1)}, u32[]{:S(2)}, u32[]{:S(2)}) %collective-permute-start.2) | collective-permute-done | bytes 262176 | tf_op jit(solution)/shard_map/ppermute | solution.py:26
  38.0 0.0 collective-permute-start.3
  38.0 0.7 convert_bitcast_fusion.1
  38.7 0.1 broadcast_bitcast_fusion
  38.8 6.0 %collective-permute-done.3 = bf16[1024,128]{1,0:T(8,128)(2,1)S(1)} collective-permute-done((bf16[1024,128]{1,0:T(8,128)(2,1)S(1)}, bf16[1024,128]{1,0:T(8,128)(2,1)S(1)}, u32[]{:S(2)}, u32[]{:S(2)}) %collective-permute-start.3) | collective-permute-done | bytes 262176 | tf_op jit(solution)/shard_map/ppermute | solution.py:26
  44.7 0.0 collective-permute-start.4
  44.7 4.5 %broadcast_multiply_fusion = bf16[16,128,1024]{2,1,0:T(8,128)(2,1)} fusion(bf16[16,128,1024]{2,1,0:T(8,128)(2,1)} %param.4, bf16[1024]{0:T(1024)(128)(2,1)S(1)} %broadcast_bitcast_fusion), kind=kLoop, calls=%fused_computation.5 | loop fusion | flops 2097152 | bytes 8390656 | tf_op jit(solution)/shard_map/mul | solution.py:37
  49.2 0.3 broadcast_in_dim.13
  49.5 0.0 copy-start
  49.5 0.1 constant_dynamic-update-slice_fusion.7
  49.6 1.9 %collective-permute-done.4 = bf16[1024,128]{1,0:T(8,128)(2,1)S(1)} collective-permute-done((bf16[1024,128]{1,0:T(8,128)(2,1)S(1)}, bf16[1024,128]{1,0:T(8,128)(2,1)S(1)}, u32[]{:S(2)}, u32[]{:S(2)}) %collective-permute-start.4) | collective-permute-done | bytes 262176 | tf_op jit(solution)/shard_map/ppermute | solution.py:26
  51.4 0.0 collective-permute-start.5
  51.4 0.1 constant_dynamic-update-slice_fusion.6
  51.5 0.1 constant_dynamic-update-slice_fusion.5
  51.6 0.1 constant_dynamic-update-slice_fusion.4
  51.7 6.4 %collective-permute-done.5 = bf16[1024,128]{1,0:T(8,128)(2,1)S(1)} collective-permute-done((bf16[1024,128]{1,0:T(8,128)(2,1)S(1)}, bf16[1024,128]{1,0:T(8,128)(2,1)S(1)}, u32[]{:S(2)}, u32[]{:S(2)}) %collective-permute-start.5) | collective-permute-done | bytes 262176 | tf_op jit(solution)/shard_map/ppermute | solution.py:26
  58.1 0.0 collective-permute-start.6
  58.1 0.1 constant_dynamic-update-slice_fusion.3
  58.2 0.1 constant_dynamic-update-slice_fusion.2
  58.3 0.1 constant_dynamic-update-slice_fusion.1
  58.4 6.4 %collective-permute-done.6 = bf16[1024,128]{1,0:T(8,128)(2,1)S(1)} collective-permute-done((bf16[1024,128]{1,0:T(8,128)(2,1)S(1)}, bf16[1024,128]{1,0:T(8,128)(2,1)S(1)}, u32[]{:S(2)}, u32[]{:S(2)}) %collective-permute-start.6) | collective-permute-done | bytes 262176 | tf_op jit(solution)/shard_map/ppermute | solution.py:26
  64.8 0.1 constant_dynamic-update-slice_fusion
  64.9 0.0 copy-done
  64.9 6.1 %fusion.10 = (bf16[16,128,1024]{2,1,0:T(8,128)(2,1)}, f32[16,128,1024]{2,1,0:T(8,128)S(1)}) fusion(bf16[16,128,1024]{2,1,0:T(8,128)(2,1)S(1)} %copy-done, bf16[1024,1024]{1,0:T(8,128)(2,1)S(1)} %constant_dynamic-update-slice_fusion), kind=kOutput, calls=%fused_computation.21 | convolution fusion | flops 4297064448 | bytes 18874368 | tf_op jit(solution)/shard_map/pmn,nk->pmk/dot_general | solution.py:40
  71.0 15.8 %fusion.5 = f32[16,16]{1,0:T(8,128)S(1)} fusion(bf16[16,128,1024]{2,1,0:T(8,128)(2,1)S(1)} %copy-done, f32[16,128,1024]{2,1,0:T(8,128)S(1)} %get-tuple-element.3), kind=kOutput, calls=%fused_computation.6 | convolution fusion | flops 402653184 | bytes 12583936 | tf_op jit(solution)/shard_map/dot_general | solution.py:45
  86.8 12.1 %psum.7 = f32[16,16]{1,0:T(8,128)S(1)} all-reduce(f32[16,16]{1,0:T(8,128)S(1)} %fusion.5), channel_id=1, replica_groups=mesh['aux'=4,'ao'=8] {'ao'}, use_global_device_ids=true, to_apply=%region_0.1 | all-reduce | flops 256 | bytes 2048 | tf_op jit(solution)/shard_map/psum | solution.py:46
  98.9 0.6 broadcast_multiply_fusion.2
Async XLA Ops:
  17.9 6.7 %collective-permute-start = (bf16[1024,128]{1,0:T(8,128)(2,1)S(1)}, bf16[1024,128]{1,0:T(8,128)(2,1)S(1)}, u32[]{:S(2)}, u32[]{:S(2)}) collective-permute-start(bf16[1024,128]{1,0:T(8,128)(2,1)S(1)} %all_gather.3), channel_id=1, source_target_pairs={{0,1},{1,2},{2,3},{3,4},{4,5},{5,6},{6,7},{7,0},{8,9},{9,10},{10,1... | collective-permute-start | bytes 786440 | tf_op jit(solution)/shard_map/ppermute | solution.py:26
  24.6 6.7 %collective-permute-start.1 = (bf16[1024,128]{1,0:T(8,128)(2,1)S(1)}, bf16[1024,128]{1,0:T(8,128)(2,1)S(1)}, u32[]{:S(2)}, u32[]{:S(2)}) collective-permute-start(bf16[1024,128]{1,0:T(8,128)(2,1)S(1)} %collective-permute-done), channel_id=1, source_target_pairs={{0,1},{1,2},{2,3},{3,4},{4,5},{5,6},{6,7},{7,0},{8,9},{9,10},{10,1... | collective-permute-start | bytes 786440 | tf_op jit(solution)/shard_map/ppermute | solution.py:26
  31.3 6.7 %collective-permute-start.2 = (bf16[1024,128]{1,0:T(8,128)(2,1)S(1)}, bf16[1024,128]{1,0:T(8,128)(2,1)S(1)}, u32[]{:S(2)}, u32[]{:S(2)}) collective-permute-start(bf16[1024,128]{1,0:T(8,128)(2,1)S(1)} %collective-permute-done.1), channel_id=1, source_target_pairs={{0,1},{1,2},{2,3},{3,4},{4,5},{5,6},{6,7},{7,0},{8,9},{9,10},{10,1... | collective-permute-start | bytes 786440 | tf_op jit(solution)/shard_map/ppermute | solution.py:26
  38.0 6.7 %collective-permute-start.3 = (bf16[1024,128]{1,0:T(8,128)(2,1)S(1)}, bf16[1024,128]{1,0:T(8,128)(2,1)S(1)}, u32[]{:S(2)}, u32[]{:S(2)}) collective-permute-start(bf16[1024,128]{1,0:T(8,128)(2,1)S(1)} %collective-permute-done.2), channel_id=1, source_target_pairs={{0,1},{1,2},{2,3},{3,4},{4,5},{5,6},{6,7},{7,0},{8,9},{9,10},{10,1... | collective-permute-start | bytes 786440 | tf_op jit(solution)/shard_map/ppermute | solution.py:26
  44.7 6.7 %collective-permute-start.4 = (bf16[1024,128]{1,0:T(8,128)(2,1)S(1)}, bf16[1024,128]{1,0:T(8,128)(2,1)S(1)}, u32[]{:S(2)}, u32[]{:S(2)}) collective-permute-start(bf16[1024,128]{1,0:T(8,128)(2,1)S(1)} %collective-permute-done.3), channel_id=1, source_target_pairs={{0,1},{1,2},{2,3},{3,4},{4,5},{5,6},{6,7},{7,0},{8,9},{9,10},{10,1... | collective-permute-start | bytes 786440 | tf_op jit(solution)/shard_map/ppermute | solution.py:26
  49.5 15.4 %copy-start = (bf16[16,128,1024]{2,1,0:T(8,128)(2,1)S(1)}, bf16[16,128,1024]{2,1,0:T(8,128)(2,1)}, u32[]{:S(2)}) copy-start(bf16[16,128,1024]{2,1,0:T(8,128)(2,1)} %broadcast_multiply_fusion) | copy-start | bytes 12582916
  51.4 6.7 %collective-permute-start.5 = (bf16[1024,128]{1,0:T(8,128)(2,1)S(1)}, bf16[1024,128]{1,0:T(8,128)(2,1)S(1)}, u32[]{:S(2)}, u32[]{:S(2)}) collective-permute-start(bf16[1024,128]{1,0:T(8,128)(2,1)S(1)} %collective-permute-done.4), channel_id=1, source_target_pairs={{0,1},{1,2},{2,3},{3,4},{4,5},{5,6},{6,7},{7,0},{8,9},{9,10},{10,1... | collective-permute-start | bytes 786440 | tf_op jit(solution)/shard_map/ppermute | solution.py:26
  58.1 6.7 %collective-permute-start.6 = (bf16[1024,128]{1,0:T(8,128)(2,1)S(1)}, bf16[1024,128]{1,0:T(8,128)(2,1)S(1)}, u32[]{:S(2)}, u32[]{:S(2)}) collective-permute-start(bf16[1024,128]{1,0:T(8,128)(2,1)S(1)} %collective-permute-done.5), channel_id=1, source_target_pairs={{0,1},{1,2},{2,3},{3,4},{4,5},{5,6},{6,7},{7,0},{8,9},{9,10},{10,1... | collective-permute-start | bytes 786440 | tf_op jit(solution)/shard_map/ppermute | solution.py:26

commit v2 on v0

--- a/solution.py
+++ b/solution.py
@@ -4,6 +4,10 @@
 from jax.sharding import PartitionSpec as P
 
 BLK = 128
+
+
+def arrange_the_classes(chip_axis, matrix):
+    return lax.all_gather(matrix, axis_name=chip_axis).sum(axis=0)
 
 
 def expand_blocks(mask, width):
@@ -24,7 +28,7 @@
     flat_product = product.reshape(aux_count, row_count * orbitals)
     flat_masked = masked.reshape(aux_count, row_count * orbitals).astype(jnp.float32)
     partial_polar = jnp.dot(flat_product, flat_masked.T, precision=lax.Precision.HIGHEST)
-    polar = lax.psum(partial_polar, "ao") / orbitals
+    polar = arrange_the_classes("ao", partial_polar) / orbitals
     return (product.astype(jnp.bfloat16), polar)
 
 

time: 102 us -> 97.4 us (0.955)
  blocking collectives: 29.7 us -> 25.5 us
    psum x1 -> x0, blocking collectives: 13.4 us -> none  [local(): polar = lax.psum(partial_polar, 'ao') / orbitals]
    all_gather x0 -> x1, blocking collectives: none -> 9.21 us  [arrange_the_classes(): return lax.all_gather(matrix, axis_name=chip_axis).sum(axis=0)]
where the time goes in v2:
time: 97.4 us; the launch traced here: 97.2 us
  blocking collectives  25.5 us (26%)
  matrix products  25.3 us (26%)
  waiting for transfers between devices  24.8 us (25%)
  between operations  14 us (14%)
  other arithmetic  7.26 us (7%)
    all_gather x1, waiting for transfers between devices, local(): lax.all_gather(columns, 'ao', axis=1, tiled=True)  24.8 us
    all_gather x1, blocking collectives, local(): columns = lax.all_gather(green_local, 'aux', axis=0, tiled=True)  16.3 us
    dot_general x1, matrix products, local(): jnp.dot(flat_product, flat_masked.T, precision=lax.Precision.HIGHEST)  15.8 us
    dot_general x1, matrix products, local(): jnp.einsum('pmn,nk->pmk', masked, lax.all_gather(columns, 'ao', axis=1, t...  9.54 us
    all_gather x1, blocking collectives, arrange_the_classes(): return lax.all_gather(matrix, axis_name=chip_axis).sum(axis=0)  9.21 us
    mul x1, other arithmetic, local(): tensor * expand_blocks(tensor_mask[0], BLK).astype(jnp.bfloat16)[None]  4.39 us
  transfers between devices with their start and end apart: 1, of which 1 were waited for; matrix products, arithmetic and copies ran while one was open for 5% of the time, Pallas kernels for 0%

profile of v2, /device:TPU:0, one launch (start us, length us, event | category | flops | bytes accessed | tf_op | source)
XLA Modules:
  0.0 97.2 jit_solution(3464120384544892419)
XLA Ops:
  7.2 0.0 all-gather.3.cloned.1.call-start
  7.2 0.7 convert_bitcast_fusion
  7.9 0.1 broadcast_bitcast_fusion.1
  7.9 0.9 broadcast_multiply_fusion.1
  8.9 16.3 %all_gather.12 = bf16[1024,128]{1,0:T(8,128)(2,1)} all-gather(bf16[256,128]{1,0:T(8,128)(2,1)S(1)} %broadcast_multiply_fusion.1), channel_id=1, replica_groups=mesh['aux'=4,'ao'=8] {'aux'}, dimensions={0}, use_global_device_ids=true | all-gather | bytes 327680 | tf_op jit(solution)/shard_map/all_gather | solution.py:21
  25.2 0.0 all-gather.3.cloned.1.call-update
  25.2 0.7 convert_bitcast_fusion.1
  25.9 0.1 broadcast_bitcast_fusion
  26.0 4.4 %broadcast_multiply_fusion = bf16[16,128,1024]{2,1,0:T(8,128)(2,1)} fusion(bf16[16,128,1024]{2,1,0:T(8,128)(2,1)} %param.4, bf16[1024]{0:T(1024)(128)(2,1)S(1)} %broadcast_bitcast_fusion), kind=kLoop, calls=%fused_computation.5 | loop fusion | flops 2097152 | bytes 8390656 | tf_op jit(solution)/shard_map/mul | solution.py:19
  30.4 24.8 %all-gather.3.cloned.1.call-done = bf16[1024,1024]{1,0:T(8,128)(2,1)} async-done(((bf16[1024,128]{1,0:T(8,128)(2,1)}), bf16[1024,1024]{1,0:T(8,128)(2,1)}) %all-gather.3.cloned.1.call-update) | async-done | bytes 2097168 | tf_op jit(solution)/shard_map/all_gather | solution.py:25
  55.1 0.0 copy-start
  55.2 9.5 %fusion.10 = (bf16[16,128,1024]{2,1,0:T(8,128)(2,1)}, f32[16,128,1024]{2,1,0:T(8,128)S(1)}) fusion(bf16[16,128,1024]{2,1,0:T(8,128)(2,1)} %broadcast_multiply_fusion, bf16[1024,1024]{1,0:T(8,128)(2,1)} %all-gather.3.cloned.1.call-done), kind=kOutput, calls=%fused_computation.13 | convolution fusion | flops 4297064448 | bytes 18874368 | tf_op jit(solution)/shard_map/pmn,nk->pmk/dot_general | solution.py:22
  64.7 0.0 copy-done
  64.7 15.8 %fusion.5 = f32[16,16]{1,0:T(8,128)S(1)} fusion(bf16[16,128,1024]{2,1,0:T(8,128)(2,1)S(1)} %copy-done, f32[16,128,1024]{2,1,0:T(8,128)S(1)} %get-tuple-element.3), kind=kOutput, calls=%fused_computation.6 | convolution fusion | flops 402653184 | bytes 12583936 | tf_op jit(solution)/shard_map/dot_general | solution.py:30
  80.5 9.2 %all-gather = f32[128,16]{1,0:T(8,128)S(1)} all-gather(f32[16,16]{1,0:T(8,128)S(1)} %fusion.5), channel_id=2, replica_groups=mesh['aux'=4,'ao'=8] {'ao'}, dimensions={0}, use_global_device_ids=true | all-gather | bytes 9216 | tf_op jit(solution)/shard_map/all_gather | solution.py:10
  89.7 0.6 broadcast_multiply_fusion.2
  (1 shorter events, 0.0 us)
Async XLA Ops:
  7.2 48.0 %all-gather.3.cloned.1.call-start = ((), (), s32[]{:S(2)}) async-start(), calls=%async_computation | async-start | bytes 2359296 | tf_op jit(solution)/shard_map/all_gather | solution.py:25
  55.1 9.5 %copy-start = (bf16[16,128,1024]{2,1,0:T(8,128)(2,1)S(1)}, bf16[16,128,1024]{2,1,0:T(8,128)(2,1)}, u32[]{:S(2)}) copy-start(bf16[16,128,1024]{2,1,0:T(8,128)(2,1)} %broadcast_multiply_fusion) | copy-start | bytes 12582916
Sparse Core Ops, SparseCore 0:
  25.3 29.7 all-gather.2
